TPU v7x, 32 devices: a whole 2x2x4 slice. The times are simulated.
32 devices in a mesh: grp: 2 (over x), seq: 16 (over z, y, core).
Axes of the slice: x: 2, y: 2, z: 4, core: 2. Of those that a mesh axis runs over, the one named last changes fastest.
Arguments:
- tokens: bfloat16 [4096, 8192], P(('grp', 'seq')), may hold values from -6 to 6
- cotangent: bfloat16 [4096, 1024], P(('grp', 'seq')), may hold values from -6 to 6
- frozen_weight: bfloat16 [8192, 1024], P('seq'), may hold values from -0.0625 to 0.0625
- adapters: bfloat16 [32, 9216, 64], P('grp', 'seq'), may hold values from -0.5 to 0.5
- tile_job: int32 [32, 1], replicated, may hold values from 0 to 31
- job_slot: int32 [32], replicated, may hold values from 0 to 31, each once
Outputs:
- keys: bfloat16 [4096, 1024], P(('grp', 'seq'))
- token_gradient: bfloat16 [4096, 8192], P(('grp', 'seq'))
- grad_adapters: float32 [32, 9216, 64], P('grp', 'seq')
All inputs are finite; a program needn't handle non-finite values.
Results may differ from a plain program's by a relative error of at most 0.0029.
Values may be sent and summed in bfloat16 or wider, within the bound.
A program may use at most 128 MiB of HBM per device.

v0:
```python
import jax
import jax.numpy as jnp
from jax import lax
from jax.sharding import PartitionSpec as P

TILE_ROWS = 128


adapter_scale = 0.5


def on_device(tokens, cotangent, frozen_weight, adapters, tile_job, job_slot):
    rank_width = tokens.shape[1]
    key_columns = cotangent.shape[1]
    rank = adapters.shape[2]
    slot_count = adapters.shape[0]
    row_count = adapters.shape[1]
    total_jobs = job_slot.shape[0]
    groups = lax.axis_size("grp")
    shards = lax.axis_size("seq")
    tiles_dev = tokens.shape[0] // TILE_ROWS
    group_index = lax.axis_index("grp")
    jobs = tile_job[:, 0]
    table = jnp.arange(total_jobs, dtype=jnp.int32)
    slots_all = jnp.sum(jnp.where(jobs[:, None] == table[None, :], job_slot[None, :], 0), axis=1)
    slots_all = slots_all.reshape(groups, shards, tiles_dev)
    group_slots = lax.dynamic_index_in_dim(slots_all, group_index, 0, keepdims=False)
    tile_slots = group_slots.T
    piece = lax.all_gather(frozen_weight, "seq", axis=0, tiled=True)
    forward_pass = jnp.dot(tokens, piece, preferred_element_type=jnp.float32)
    weight_update = jnp.einsum("nk,dk->nd", cotangent, piece, preferred_element_type=jnp.float32)
    owners = jnp.transpose(slots_all // slot_count, (0, 2, 1))
    local_slots = jnp.transpose(slots_all % slot_count, (0, 2, 1))
    picked = jnp.take(adapters, local_slots, axis=0)
    outgoing = jnp.where((owners == group_index)[..., None, None], picked, jnp.zeros_like(picked))
    arrived = lax.all_to_all(
        lax.all_to_all(outgoing, "grp", split_axis=0, concat_axis=0, tiled=True),
        "seq",
        split_axis=2,
        concat_axis=2,
        tiled=True,
    )
    fetched = jnp.sum(arrived.astype(jnp.float32), axis=0).astype(jnp.bfloat16)
    adapter_full = fetched.reshape(tiles_dev, shards * row_count, rank)
    down_weight = adapter_full[:, :rank_width]
    up_weight = adapter_full[:, rank_width:]
    token_tiles = tokens.reshape(tiles_dev, TILE_ROWS, rank_width)
    cot_tiles = cotangent.reshape(tiles_dev, TILE_ROWS, key_columns)
    hidden_width = jnp.einsum(
        "tnd,tdr->tnr", token_tiles, down_weight, preferred_element_type=jnp.float32
    ).astype(jnp.bfloat16)
    adapter_weights = jnp.einsum(
        "mhw,mow->mho", hidden_width, up_weight, preferred_element_type=jnp.float32
    )
    keys = (forward_pass + adapter_scale * adapter_weights.reshape(-1, key_columns)).astype(
        jnp.bfloat16
    )
    backward_pass = jnp.einsum(
        "tnk,tkr->tnr", cot_tiles, up_weight, preferred_element_type=jnp.float32
    ).astype(jnp.bfloat16)
    pass_through = jnp.einsum(
        "tnr,tdr->tnd", backward_pass, down_weight, preferred_element_type=jnp.float32
    )
    token_gradient = (weight_update + adapter_scale * pass_through.reshape(-1, rank_width)).astype(
        jnp.bfloat16
    )
    down_term = adapter_scale * jnp.einsum(
        "tnd,tnr->tdr", token_tiles, backward_pass, preferred_element_type=jnp.float32
    )
    up_term = adapter_scale * jnp.einsum(
        "tnk,tnr->tkr", cot_tiles, hidden_width, preferred_element_type=jnp.float32
    )
    terms = jnp.concatenate([down_term, up_term], axis=1).reshape(
        tiles_dev, shards, row_count, rank
    )
    incoming = lax.all_to_all(terms, "seq", split_axis=1, concat_axis=1, tiled=True)
    selector = (tile_slots.reshape(-1)[None, :] == table[:, None]).astype(jnp.float32)
    sums = jnp.dot(
        selector,
        incoming.reshape(tiles_dev * shards, row_count * rank),
        precision=lax.Precision.HIGHEST,
        preferred_element_type=jnp.float32,
    )
    owned = lax.psum_scatter(
        sums.reshape(total_jobs, row_count, rank), "grp", scatter_dimension=0, tiled=True
    )
    return (keys, token_gradient, owned)


def solution(mesh):
    placed = (
        P(("grp", "seq"), None),
        P(("grp", "seq"), None),
        P("seq", None),
        P("grp", "seq", None),
        P(),
        P(),
    )
    return jax.shard_map(
        on_device,
        mesh=mesh,
        in_specs=placed,
        out_specs=(P(("grp", "seq"), None), P(("grp", "seq"), None), P("grp", "seq", None)),
        check_vma=False,
    )
```

profile of v0, /device:TPU:0, one launch (start us, length us, event | category | flops | bytes accessed | tf_op | source)
XLA Modules:
  0.0 384.9 jit_solution(4573344072761720430)
XLA Ops:
  8.0 1.0 select_reduce_fusion
  9.2 0.4 copy-done.3
  9.7 3.7 gather_fusion
  13.4 2.2 select_select_fusion
  15.6 34.5 %all_to_all.15 = bf16[2,1,16,576,64]{3,4,2,1,0:T(8,128)(2,1)S(1)} all-to-all(bf16[2,1,16,576,64]{3,4,2,1,0:T(8,128)(2,1)S(1)} %select_select_fusion), channel_id=1, replica_groups=mesh['grp'=2,'seq'=16] {'grp'}, dimensions={0} | all-to-all | bytes 4718592 | tf_op jit(solution)/shard_map/all_to_all | solution.py:37
  50.4 64.6 %all_to_all.16 = bf16[2,1,16,576,64]{3,4,0,1,2:T(8,128)(2,1)} all-to-all(bf16[2,1,16,576,64]{3,4,0,1,2:T(8,128)(2,1)S(1)} %copy.26), channel_id=1, replica_groups=mesh['grp'=2,'seq'=16] {'seq'}, dimensions={2} | all-to-all | bytes 4718592 | tf_op jit(solution)/shard_map/all_to_all | solution.py:36
  115.1 2.4 reduce_sum.22
  117.4 1.8 copy.28
  119.2 2.4 reshape.282
  121.6 1.2 convolution_convert_fusion.1
  122.8 0.8 convolution_convert_fusion
  123.8 0.4 fusion.2
  124.3 1.6 pad_maximum_fusion
  125.9 3.2 reshape.286
  129.1 4.1 %copy.29 = f32[1,16,576,64]{2,3,0,1:T(8,128)} copy(f32[1,16,576,64]{2,1,3,0:T(8,128)} %reshape.286) | data formatting | bytes 4718592 | tf_op jit(solution)/shard_map/reshape | solution.py:73
  133.2 5.2 %all-to-all-start.2 = ((f32[1,16,576,64]{2,3,0,1:T(8,128)}), f32[1,16,576,64]{2,3,0,1:T(8,128)}, u32[]{:S(2)}, u32[]{:S(2)}) async-start(f32[1,16,576,64]{2,3,0,1:T(8,128)} %copy.29), calls=%async_computation.2 | async-start | bytes 5242880 | tf_op jit(solution)/shard_map/all_to_all | solution.py:76
  138.4 1.3 reshape.285
  139.8 1.2 dynamic-slice_bitcast_fusion
  141.0 47.7 %all-to-all-done.2 = f32[1,16,576,64]{2,3,0,1:T(8,128)} async-done(((f32[1,16,576,64]{2,3,0,1:T(8,128)}), f32[1,16,576,64]{2,3,0,1:T(8,128)}, u32[]{:S(2)}, u32[]{:S(2)}) %all-to-all-start.2) | async-done | bytes 2359328 | tf_op jit(solution)/shard_map/all_to_all | solution.py:76
  188.7 4.8 %copy.30 = f32[1,16,576,64]{3,2,1,0:T(8,128)} copy(f32[1,16,576,64]{2,3,0,1:T(8,128)} %all-to-all-done.2) | data formatting | bytes 4718592 | tf_op jit(solution)/shard_map/all_to_all | solution.py:76
  193.5 4.1 %reshape.287 = f32[16,36864]{1,0:T(8,128)} reshape(f32[1,16,576,64]{3,2,1,0:T(8,128)} %copy.30) | data formatting | bytes 4718592 | tf_op jit(solution)/shard_map/reshape | solution.py:80
  197.7 4.6 %dot_general.40 = f32[576,64,16]{1,0,2:T(8,128)} reshape(f32[36864,16]{0,1:T(8,128)} %bitcast.48) | data formatting | bytes 4718592 | tf_op jit(solution)/shard_map/dot_general | solution.py:78
  202.2 5.4 %copy.31 = f32[576,64,16]{0,2,1:T(8,128)} copy(f32[576,64,16]{1,0,2:T(8,128)} %dot_general.40) | data formatting | bytes 4718592 | tf_op jit(solution)/shard_map/dot_general | solution.py:78
  207.6 6.4 %fusion.7 = f32[32,576,64]{1,0,2:T(8,128)} fusion(f32[576,64,16]{0,2,1:T(8,128)} %copy.31, s32[16]{0:T(128)} %dynamic-slice_bitcast_fusion), kind=kOutput, calls=%fused_computation.21 | convolution fusion | flops 226492928 | bytes 7077952 | tf_op jit(solution)/shard_map/dot_general | solution.py:78
  214.2 0.3 all-gather.2.cloned.1.call-update
  214.6 73.0 %reduce-scatter.2.cloned.1.call-done = f32[16,576,64]{1,0,2:T(8,128)} async-done(((f32[32,576,64]{1,0,2:T(8,128)}), f32[16,576,64]{1,0,2:T(8,128)}) %reduce-scatter.2.cloned.1.call-update) | async-done | bytes 2359312 | tf_op jit(solution)/shard_map/reduce_scatter | solution.py:84
  287.6 4.1 %copy.32 = f32[16,576,64]{1,2,0:T(8,128)} copy(f32[16,576,64]{1,0,2:T(8,128)} %reduce-scatter.2.cloned.1.call-done) | data formatting | bytes 4718592
  291.7 59.2 %all-gather.2.cloned.1.call-done = bf16[8192,1024]{1,0:T(8,128)(2,1)} async-done(((bf16[512,1024]{1,0:T(8,128)(2,1)}), bf16[8192,1024]{1,0:T(8,128)(2,1)}) %all-gather.2.cloned.1.call-update) | async-done | bytes 16777232 | tf_op jit(solution)/shard_map/all_gather | solution.py:29
  350.9 13.3 %fusion.13 = f32[128,8192]{1,0:T(8,128)} fusion(bf16[128,1024]{1,0:T(8,128)(2,1)S(1)} %copy-done.1, bf16[8192,1024]{1,0:T(8,128)(2,1)} %all-gather.2.cloned.1.call-done), kind=kOutput, calls=%fused_computation.41 | convolution fusion | flops 2147483648 | bytes 21233664 | tf_op jit(solution)/shard_map/nk,dk->nd/dot_general | solution.py:31
  364.1 4.3 %fusion.1 = bf16[128,8192]{1,0:T(8,128)(2,1)} fusion(f32[128,8192]{1,0:T(8,128)} %fusion.13, bf16[64,128]{1,0:T(8,128)(2,1)} %copy-done.2, bf16[1,9216,64]{1,2,0:T(8,128)(2,1)S(1)} %reshape.282), kind=kOutput, calls=%fused_computation.3 | convolution fusion | flops 137363456 | bytes 7356416 | tf_op jit(solution)/shard_map/tnr,tdr->tnd/dot_general | solution.py:61
  368.4 8.1 %fusion.12 = f32[128,1024]{1,0:T(8,128)S(1)} fusion(bf16[128,8192]{1,0:T(8,128)(2,1)S(1)} %copy-done, bf16[8192,1024]{1,0:T(8,128)(2,1)} %all-gather.2.cloned.1.call-done), kind=kOutput, calls=%fused_computation.40 | convolution fusion | flops 2147483648 | bytes 19398656 | tf_op jit(solution)/shard_map/dot_general | solution.py:30
  376.5 1.0 fusion.4
  (18 shorter events, 1.0 us)
Async XLA Ops:
  8.0 114.8 %copy-start = (bf16[128,8192]{1,0:T(8,128)(2,1)S(1)}, bf16[128,8192]{1,0:T(8,128)(2,1)}, u32[]{:S(2)}) copy-start(bf16[128,8192]{1,0:T(8,128)(2,1)} %param.6) | copy-start | bytes 6291460
  9.0 0.6 copy-start.3
  119.2 4.4 %copy-start.1 = (bf16[128,1024]{1,0:T(8,128)(2,1)S(1)}, bf16[128,1024]{1,0:T(8,128)(2,1)}, u32[]{:S(2)}) copy-start(bf16[128,1024]{1,0:T(8,128)(2,1)} %param.7) | copy-start | bytes 786436
  122.8 1.1 copy-start.2
  133.2 55.5 %all-to-all-start.2 = ((f32[1,16,576,64]{2,3,0,1:T(8,128)}), f32[1,16,576,64]{2,3,0,1:T(8,128)}, u32[]{:S(2)}, u32[]{:S(2)}) async-start(f32[1,16,576,64]{2,3,0,1:T(8,128)} %copy.29), calls=%async_computation.2 | async-start | bytes 5242880 | tf_op jit(solution)/shard_map/all_to_all | solution.py:76
  138.4 149.2 %reduce-scatter.2.cloned.1.call-start = ((), (), s32[]{:S(2)}) async-start(), calls=%async_computation.5 | async-start | bytes 7864320 | tf_op jit(solution)/shard_map/reduce_scatter | solution.py:84
  214.0 136.8 %all-gather.2.cloned.1.call-start = ((), (), s32[]{:S(2)}) async-start(), calls=%async_computation.4 | async-start | bytes 17825792 | tf_op jit(solution)/shard_map/all_gather | solution.py:29
Sparse Core Ops, SparseCore 0:
  214.1 73.3 reduce-scatter.1
Sparse Core Ops, SparseCore 1:
  216.7 134.2 all-gather.1
where the time goes:
time: 386 us; the launch traced here: 385 us
  waiting for transfers between devices  180 us (47%)
  blocking collectives  99.2 us (26%)
  local copies, waits for them, and re-layouts  41.7 us (11%)
  matrix products  35.5 us (9%)
  between operations  15.6 us (4%)
  other arithmetic  7.2 us (2%)
  starting transfers between devices  5.45 us (1%)
    reduce_scatter x1, waiting for transfers between devices, on_device(): lax.psum_scatter(sums.reshape(total_jobs, row_count, rank), 'grp', scatte...  73 us
    all_to_all x1, blocking collectives, on_device(): lax.all_to_all(lax.all_to_all(outgoing, 'grp', split_axis=0, concat_axis=...  64.6 us
    all_gather x1, waiting for transfers between devices, on_device(): piece = lax.all_gather(frozen_weight, 'seq', axis=0, tiled=True)  59.2 us
    all_to_all x1, waiting for transfers between devices, on_device(): lax.all_to_all(terms, 'seq', split_axis=1, concat_axis=1, tiled=True)  47.7 us
    all_to_all x1, blocking collectives, on_device(): lax.all_to_all(outgoing, 'grp', split_axis=0, concat_axis=0, tiled=True)  34.5 us
    dot_general x1, matrix products, on_device(): jnp.einsum('nk,dk->nd', cotangent, piece, preferred_element_type=jnp.floa...  13.3 us
    dot_general x2, local copies, waits for them, and re-layouts, on_device(): jnp.dot(selector, incoming.reshape(tiles_dev * shards, row_count * rank),...  9.98 us
    dot_general x1, matrix products, on_device(): forward_pass = jnp.dot(tokens, piece, preferred_element_type=jnp.float32)  8.09 us
  transfers between devices with their start and end apart: 3, of which 3 were waited for; matrix products, arithmetic and copies ran while one was open for 2% of the time, Pallas kernels for 0%

commit v1 on v0

--- a/solution.py
+++ b/solution.py
@@ -1,12 +1,323 @@
+import functools
+
 import jax
 import jax.numpy as jnp
 from jax import lax
+from jax.experimental import pallas as pl
+from jax.experimental.pallas import tpu as pltpu
 from jax.sharding import PartitionSpec as P
 
 TILE_ROWS = 128
-
+MESH = pl.DeviceIdType.MESH
 
 adapter_scale = 0.5
+
+PLANES = 4
+SHARDS = 16
+
+
+def nt_dot(a, b):
+    return lax.dot_general(a, b, (((1,), (1,)), ((), ())), preferred_element_type=jnp.float32)
+
+
+def dot(a, b):
+    return jnp.dot(a, b, preferred_element_type=jnp.float32)
+
+
+def exchange_kernel(
+    slots_ref, tok_ref, cot_ref, w_ref, adp_ref,
+    keys_ref, tg_ref, gbuf,
+    wbuf, all_adp, picked, pieces, down_t, gsend, acc, back,
+    w_send, w_recv, own_sem, xa_send, xa_recv, a_send, a_recv, g_send, g_recv, xg_send, xg_recv,
+):
+    grp = lax.axis_index("grp")
+    me = lax.axis_index("seq")
+    core = me % 2
+    row = (me // 2) % 2
+    plane = me // 4
+    slot_count, rank, piece_cols = adp_ref.shape
+    width = tok_ref.shape[1]
+    shard_rows = width // SHARDS
+
+    barrier = pltpu.get_barrier_semaphore()
+    def greet(p, _):
+        pl.semaphore_signal(barrier, inc=1, device_id=(grp, (me + p) % SHARDS), device_id_type=MESH)
+        return 0
+    own_copies = [
+        pltpu.make_async_copy(w_ref.at[h], wbuf.at[me, h], w_recv.at[me * 2 + h]) for h in range(2)
+    ]
+    for copy in own_copies:
+        copy.start()
+    keep = pltpu.make_async_copy(adp_ref, all_adp.at[pl.ds(grp * slot_count, slot_count)], own_sem)
+    keep.start()
+    lax.fori_loop(1, SHARDS, greet, 0)
+    pl.semaphore_signal(barrier, inc=1, device_id=(1 - grp, me), device_id_type=MESH)
+    pl.semaphore_wait(barrier, SHARDS)
+
+    def adapter_swap():
+        return pltpu.make_async_remote_copy(
+            adp_ref, all_adp.at[pl.ds(grp * slot_count, slot_count)], xa_send, xa_recv,
+            device_id=(1 - grp, me), device_id_type=MESH)
+
+    adapter_swap().start()
+
+    def send_w(p, y, h, kind):
+        s = p * 4 + y * 2 + core
+        target = (
+            (grp, me + 4), (grp, me - 4),
+            (grp, plane * 4 + (1 - row) * 2 + core),
+            (1 - grp, me),
+            (grp, plane * 4 + row * 2 + 1 - core),
+        )[kind]
+        return pltpu.make_async_remote_copy(
+            wbuf.at[s, h], wbuf.at[s, h],
+            w_send.at[((p * 2 + y) * 2 + h) * 5 + kind], w_recv.at[s * 2 + h],
+            device_id=target, device_id_type=MESH)
+
+    def take_w(s, h):
+        pltpu.make_async_copy(wbuf.at[s, h], wbuf.at[s, h], w_recv.at[s * 2 + h]).wait()
+
+    def with_plane(k, do):
+        d = (k + 1) // 2
+        p = plane + d * (2 * (k % 2) - 1)
+        pl.when((k >= 0) & (k < 2 * PLANES - 1) & (p >= 0) & (p < PLANES))(functools.partial(do, p))
+
+    def along_planes(p, h, act):
+        @pl.when((p <= plane) & (plane < PLANES - 1))
+        def _():
+            act(send_w(p, row, h, 0))
+
+        @pl.when((p >= plane) & (plane > 0))
+        def _():
+            act(send_w(p, row, h, 1))
+
+    def start(copy):
+        copy.start()
+
+    def finish(copy):
+        copy.wait_send()
+
+    def plane_step(p):
+        for h in range(2):
+            take_w(p * 4 + row * 2 + core, h)
+            along_planes(p, h, start)
+
+            @pl.when(grp == h)
+            def _():
+                send_w(p, row, h, 2).start()
+
+            send_w(p, row, h, 4).start()
+
+    def row_step(p):
+        take_w(p * 4 + (1 - row) * 2 + core, grp)
+        send_w(p, 1 - row, grp, 3).start()
+        send_w(p, 1 - row, grp, 4).start()
+
+    def group_step(p):
+        take_w(p * 4 + (1 - row) * 2 + core, 1 - grp)
+        send_w(p, 1 - row, 1 - grp, 4).start()
+
+    def core_step(p):
+        for y in range(2):
+            for h in range(2):
+                take_w(p * 4 + y * 2 + 1 - core, h)
+
+    def drain_step(p):
+        for h in range(2):
+            along_planes(p, h, finish)
+
+            @pl.when(grp == h)
+            def _():
+                send_w(p, row, h, 2).wait_send()
+
+            send_w(p, row, h, 4).wait_send()
+        send_w(p, 1 - row, grp, 3).wait_send()
+        send_w(p, 1 - row, grp, 4).wait_send()
+        send_w(p, 1 - row, 1 - grp, 4).wait_send()
+
+    def compute_step(p):
+        def shard(i, _):
+            s = p * 4 + i
+            cols = pl.ds(pl.multiple_of(s * shard_rows, shard_rows), shard_rows)
+            block = wbuf[s].reshape(shard_rows, cot_ref.shape[1])
+            acc[...] += dot(tok_ref[:, cols], block)
+            grad = nt_dot(cot_ref[...], block) + adapter_scale * dot(back[...], down_t[:, cols])
+            tg_ref[:, cols] = grad.astype(jnp.bfloat16)
+            return 0
+
+        lax.fori_loop(0, 4, shard, 0)
+
+    def send_piece(k):
+        return pltpu.make_async_remote_copy(
+            picked.at[k], pieces.at[me], a_send.at[k], a_recv.at[me],
+            device_id=(grp, k), device_id_type=MESH)
+
+    def send_term(k):
+        return pltpu.make_async_remote_copy(
+            gsend.at[k], gbuf.at[grp * SHARDS + me], g_send.at[k], g_recv.at[me],
+            device_id=(grp, k), device_id_type=MESH)
+
+    def swap_term(k):
+        return pltpu.make_async_remote_copy(
+            gbuf.at[grp * SHARDS + k], gbuf.at[grp * SHARDS + k], xg_send.at[k], xg_recv.at[k],
+            device_id=(1 - grp, me), device_id_type=MESH)
+
+    def each_peer(do):
+        def one(p, _):
+            do((me + p) % SHARDS)
+            return 0
+        lax.fori_loop(1, SHARDS, one, 0)
+
+    def pick():
+        keep.wait()
+        adapter_swap().wait_recv()
+
+        def one(t, _):
+            picked[t] = all_adp[slots_ref[grp * SHARDS + t]]
+            return 0
+
+        lax.fori_loop(0, SHARDS, one, 0)
+        each_peer(lambda k: send_piece(k).start())
+        pieces[me] = picked[me]
+
+    def adapt():
+        each_peer(lambda k: pltpu.make_async_copy(pieces.at[k], pieces.at[k], a_recv.at[k]).wait())
+        pair = 2 * piece_cols
+        for m in range(SHARDS // 2):
+            down_t[:, m * pair:(m + 1) * pair] = jnp.concatenate([pieces[2 * m], pieces[2 * m + 1]], axis=1)
+        up = down_t[:, width:]
+        hidden = jnp.zeros((TILE_ROWS, rank), jnp.float32)
+        hidden_t = jnp.zeros((rank, TILE_ROWS), jnp.float32)
+        step = width // 4
+        for q in range(4):
+            t_cols = tok_ref[:, q * step:(q + 1) * step]
+            d_cols = down_t[:, q * step:(q + 1) * step]
+            hidden = hidden + nt_dot(t_cols, d_cols)
+            hidden_t = hidden_t + nt_dot(d_cols, t_cols)
+        hidden = hidden.astype(jnp.bfloat16)
+        hidden_t = hidden_t.astype(jnp.bfloat16)
+        back[...] = nt_dot(cot_ref[...], up).astype(jnp.bfloat16)
+        back_t = nt_dot(up, cot_ref[...]).astype(jnp.bfloat16)
+        acc[...] = adapter_scale * dot(hidden, up)
+        for m in range(SHARDS // 2):
+            first, last = m * pair, (m + 1) * pair
+            if last <= width:
+                term = dot(back_t, tok_ref[:, first:last])
+            else:
+                term = jnp.concatenate(
+                    [dot(back_t, tok_ref[:, first:width]), dot(hidden_t, cot_ref[:, :last - width])], axis=1)
+            term = adapter_scale * term
+            gsend[2 * m] = term[:, :piece_cols].astype(jnp.bfloat16)
+            gsend[2 * m + 1] = term[:, piece_cols:].astype(jnp.bfloat16)
+        each_peer(lambda k: send_term(k).start())
+        gbuf[grp * SHARDS + me] = gsend[me]
+        swap_term(me).start()
+
+    def hand_on():
+        def one(k):
+            pltpu.make_async_copy(gbuf.at[grp * SHARDS + k], gbuf.at[grp * SHARDS + k], g_recv.at[k]).wait()
+            swap_term(k).start()
+        each_peer(one)
+
+    lags = (0, 1, 2, 3, 5)
+
+    def turn(j, _):
+        with_plane(j - lags[0], plane_step)
+        with_plane(j - lags[1], row_step)
+        with_plane(j - lags[2], group_step)
+        with_plane(j - lags[3], core_step)
+        pl.when(j == 2)(pick)
+        pl.when(j == 4)(adapt)
+        pl.when(j == 6)(hand_on)
+        with_plane(j - lags[4], compute_step)
+        return 0
+
+    lax.fori_loop(0, 2 * PLANES - 1 + lags[4], turn, 0)
+    keys_ref[...] = acc[...].astype(jnp.bfloat16)
+
+    def drain(k, _):
+        with_plane(k, drain_step)
+        return 0
+
+    lax.fori_loop(0, 2 * PLANES - 1, drain, 0)
+    adapter_swap().wait_send()
+    each_peer(lambda k: send_piece(k).wait_send())
+    each_peer(lambda k: send_term(k).wait_send())
+
+    def swapped(k, _):
+        other = gbuf.at[(1 - grp) * SHARDS + k]
+        swap_term(k).wait_send()
+        pltpu.make_async_copy(other, other, xg_recv.at[k]).wait()
+        return 0
+
+    lax.fori_loop(0, SHARDS, swapped, 0)
+
+
+def sum_kernel(local_ref, term_ref, out_ref):
+    out_ref[...] = jnp.zeros_like(out_ref)
+    slot_count = out_ref.shape[0]
+
+    def one(t, _):
+        slot = local_ref[t]
+
+        @pl.when((slot >= 0) & (slot < slot_count))
+        def _():
+            out_ref[slot] += term_ref[t].astype(jnp.float32)
+
+        return 0
+
+    lax.fori_loop(0, term_ref.shape[0], one, 0)
+
+
+def on_block(tokens, cotangent, frozen_weight, adapters, tile_job, job_slot):
+    table = jnp.arange(job_slot.shape[0], dtype=jnp.int32)
+    slots = jnp.sum(jnp.where(tile_job == table[None, :], job_slot[None, :], 0), axis=1).astype(jnp.int32)
+    adapters_t = jnp.swapaxes(adapters, 1, 2)
+    slot_count, rank, piece_cols = adapters_t.shape
+    tiles = slots.shape[0]
+    rows, width = tokens.shape
+    key_columns = cotangent.shape[1]
+    shard_rows = frozen_weight.shape[0]
+    halves = frozen_weight.reshape(2, shard_rows // 2, key_columns)
+    vmem = pl.BlockSpec(memory_space=pltpu.VMEM)
+    smem = pl.BlockSpec(memory_space=pltpu.SMEM)
+    bf16 = jnp.bfloat16
+    dma = pltpu.SemaphoreType.DMA
+    keys, token_gradient, terms = pl.pallas_call(
+        exchange_kernel,
+        out_shape=(
+            jax.ShapeDtypeStruct((rows, key_columns), bf16),
+            jax.ShapeDtypeStruct((rows, width), bf16),
+            jax.ShapeDtypeStruct((tiles, rank, piece_cols), bf16),
+        ),
+        in_specs=[smem, vmem, vmem, pl.BlockSpec(memory_space=pl.ANY), vmem],
+        out_specs=(vmem, vmem, vmem),
+        scratch_shapes=[
+            pltpu.VMEM((SHARDS, 2, shard_rows // 2, key_columns), bf16),
+            pltpu.VMEM((tiles, rank, piece_cols), bf16),
+            pltpu.VMEM((SHARDS, rank, piece_cols), bf16),
+            pltpu.VMEM((SHARDS, rank, piece_cols), bf16),
+            pltpu.VMEM((rank, SHARDS * piece_cols), bf16),
+            pltpu.VMEM((SHARDS, rank, piece_cols), bf16),
+            pltpu.VMEM((rows, key_columns), jnp.float32),
+            pltpu.VMEM((rows, rank), bf16),
+            dma((SHARDS * 5,)), dma((2 * SHARDS,)), dma, dma, dma,
+            dma((SHARDS,)), dma((SHARDS,)), dma((SHARDS,)), dma((SHARDS,)), dma((SHARDS,)), dma((SHARDS,)),
+        ],
+        compiler_params=pltpu.CompilerParams(
+            collective_id=0, has_side_effects=True, vmem_limit_bytes=50 * 1024 * 1024),
+        name="exchange",
+    )(slots, tokens, cotangent, halves, adapters_t)
+    local = slots - lax.axis_index("grp") * slot_count
+    grads = pl.pallas_call(
+        sum_kernel,
+        out_shape=jax.ShapeDtypeStruct((slot_count, rank, piece_cols), jnp.float32),
+        in_specs=[smem, vmem],
+        out_specs=vmem,
+        compiler_params=pltpu.CompilerParams(vmem_limit_bytes=24 * 1024 * 1024),
+        name="slot_sums",
+    )(local, terms)
+    return keys, token_gradient, jnp.swapaxes(grads, 1, 2)
 
 
 def on_device(tokens, cotangent, frozen_weight, adapters, tile_job, job_slot):
@@ -96,8 +407,9 @@
         P(),
         P(),
     )
+    laid_out = mesh.shape["grp"] == 2 and mesh.shape["seq"] == SHARDS
     return jax.shard_map(
-        on_device,
+        on_block if laid_out else on_device,
         mesh=mesh,
         in_specs=placed,
         out_specs=(P(("grp", "seq"), None), P(("grp", "seq"), None), P("grp", "seq", None)),

time: 386 us -> 183 us (0.47)
  waiting for transfers between devices: 180 us -> 0 us
  Pallas kernels: 0 us -> 174 us
  blocking collectives: 99.2 us -> 0 us
  matrix products: 35.5 us -> 0 us
  local copies, waits for them, and re-layouts: 41.7 us -> 7.25 us
  between operations: 15.6 us -> 0.67 us
  other arithmetic: 7.2 us -> 0.86 us
  starting transfers between devices: 5.45 us -> 0 us
    pallas_call x0 -> x2, Pallas kernels: none -> 174 us  [the longest x1 171 us: on_block(): pl.pallas_call(exchange_kernel, out_shape=(jax.ShapeDtypeStruct((rows, ke...]
    all_to_all x2 -> x0, blocking collectives: 99.2 us -> none  [the longest x1 64.6 us: on_device(): lax.all_to_all(lax.all_to_all(outgoing, 'grp', split_axis=0, concat_axis=...]
    reduce_scatter x1 -> x0, waiting for transfers between devices: 73 us -> none  [on_device(): lax.psum_scatter(sums.reshape(total_jobs, row_count, rank), 'grp', scatte...]
    all_gather x1 -> x0, waiting for transfers between devices: 59.2 us -> none  [on_device(): piece = lax.all_gather(frozen_weight, 'seq', axis=0, tiled=True)]
    all_to_all x1 -> x0, waiting for transfers between devices: 47.7 us -> none  [on_device(): lax.all_to_all(terms, 'seq', split_axis=1, concat_axis=1, tiled=True)]
    dot_general x9 -> x0, matrix products: 35.5 us -> none  [the longest x1 13.3 us: on_device(): jnp.einsum('nk,dk->nd', cotangent, piece, preferred_element_type=jnp.floa...]
    reshape x7 -> x0, local copies, waits for them, and re-layouts: 15.3 us -> none  [the longest x2 7.3 us: on_device(): jnp.concatenate([down_term, up_term], axis=1)]
    dot_general x2 -> x0, local copies, waits for them, and re-layouts: 9.98 us -> none  [on_device(): jnp.dot(selector, incoming.reshape(tiles_dev * shards, row_count * rank),...]
  transfers between devices with their start and end apart: 3 -> 0, of which waited for: 3 -> 0; matrix products, arithmetic and copies ran while one was open for 2% -> 0% of each run, Pallas kernels for 0% -> 0%
where the time goes in v1:
time: 183 us; the launch traced here: 182 us
  Pallas kernels  174 us (95%)
  local copies, waits for them, and re-layouts  7.25 us (4%)
    pallas_call x1, Pallas kernels, on_block(): pl.pallas_call(exchange_kernel, out_shape=(jax.ShapeDtypeStruct((rows, ke...  171 us
    unnamed x12, local copies, waits for them, and re-layouts  7.25 us

profile of v1, /device:TPU:0, one launch (start us, length us, event | category | flops | bytes accessed | tf_op | source)
XLA Modules:
  0.0 182.4 jit_solution(8635906837343792543)
XLA Ops:
  0.6 0.9 select_reduce_fusion.slots_ref
  1.5 0.0 copy-start.1
  1.5 1.3 copy-done.1
  2.8 0.0 copy-start.2
  2.8 1.2 copy-done.2
  4.0 0.0 copy-start.3
  4.0 0.9 copy-done.3
  5.0 170.7 %exchange.1 = (bf16[128,1024]{1,0:T(8,128)(2,1)S(1)}, bf16[128,8192]{1,0:T(8,128)(2,1)}, bf16[32,64,576]{2,1,0:T(8,128)(2,1)}) custom-call(s32[32]{0:T(128)S(1)} %select_reduce_fusion.slots_ref, bf16[128,8192]{1,0:T(8,128)(2,1)} %tok_ref.1, bf16[128,1024]{1,0:T(8,128)(2,1)S(1)} %copy-done.3, bf16[2,256,1024]{2,1,0:T(8,128)(2,1)S(1)} %bitcast.5, ...), custom_call_target="tpu_custom_call" | custom-call | tf_op jit(solution)/shard_map/exchange/pallas_call | solution.py:286
  175.7 0.0 copy-start
  175.7 1.7 copy-done
  177.5 0.0 copy-start.4
  177.5 2.9 %slot_sums.1 = f32[16,64,576]{2,1,0:T(8,128)} custom-call(s32[32]{0:T(128)S(1)} %broadcast_subtract_fusion.local_ref, bf16[32,64,576]{2,1,0:T(8,128)(2,1)S(1)} %copy-done), custom_call_target="tpu_custom_call" | custom-call | tf_op jit(solution)/shard_map/slot_sums/pallas_call | solution.py:312
  180.3 0.7 copy.11
  181.0 0.0 copy-done.4
  181.1 1.3 copy.12
  (1 shorter events, 0.0 us)
Async XLA Ops:
  1.5 1.3 copy-start.1
  2.8 1.2 copy-start.2
  4.0 0.9 copy-start.3
  175.7 1.7 copy-start
  177.5 3.6 %copy-start.4 = (bf16[128,8192]{1,0:T(8,128)(2,1)S(1)}, bf16[128,8192]{1,0:T(8,128)(2,1)}, u32[]{:S(2)}) copy-start(bf16[128,8192]{1,0:T(8,128)(2,1)} %get-tuple-element.13) | copy-start | bytes 6291460

commit v2 on v1

--- a/solution.py
+++ b/solution.py
@@ -25,9 +25,10 @@
 
 
 def exchange_kernel(
-    slots_ref, tok_ref, cot_ref, w_ref, adp_ref,
+    local_ref, owned_ref, tok_hbm, cot_hbm, w_ref, adp_hbm,
     keys_ref, tg_ref, gbuf,
-    wbuf, all_adp, picked, pieces, down_t, gsend, acc, back,
+    tok_ref, cot_ref, adp_ref,
+    wbuf, lent, borrowed, picked, pieces, down_t, gsend, acc, back,
     w_send, w_recv, own_sem, xa_send, xa_recv, a_send, a_recv, g_send, g_recv, xg_send, xg_recv,
 ):
     grp = lax.axis_index("grp")
@@ -35,7 +36,7 @@
     core = me % 2
     row = (me // 2) % 2
     plane = me // 4
-    slot_count, rank, piece_cols = adp_ref.shape
+    rank, piece_cols = adp_ref.shape[1:]
     width = tok_ref.shape[1]
     shard_rows = width // SHARDS
 
@@ -46,20 +47,34 @@
     own_copies = [
         pltpu.make_async_copy(w_ref.at[h], wbuf.at[me, h], w_recv.at[me * 2 + h]) for h in range(2)
     ]
-    for copy in own_copies:
+    adp_copy = pltpu.make_async_copy(adp_hbm, adp_ref, own_sem.at[0])
+    tok_copy = pltpu.make_async_copy(tok_hbm, tok_ref, own_sem.at[1])
+    cot_copy = pltpu.make_async_copy(cot_hbm, cot_ref, own_sem.at[2])
+    for copy in (adp_copy, *own_copies, tok_copy, cot_copy):
         copy.start()
-    keep = pltpu.make_async_copy(adp_ref, all_adp.at[pl.ds(grp * slot_count, slot_count)], own_sem)
-    keep.start()
     lax.fori_loop(1, SHARDS, greet, 0)
     pl.semaphore_signal(barrier, inc=1, device_id=(1 - grp, me), device_id_type=MESH)
+    adp_copy.wait()
+
+    def each_peer(do, away=1):
+        def one(p, _):
+            do((me + away * p) % SHARDS)
+            return 0
+        lax.fori_loop(1, SHARDS, one, 0)
+
+    def lend(t):
+        return pltpu.make_async_remote_copy(
+            lent.at[t], borrowed.at[t], xa_send.at[t], xa_recv.at[t],
+            device_id=(1 - grp, me), device_id_type=MESH)
+
+    def pick_lent(t, _):
+        lent[t] = adp_ref[local_ref[(1 - grp) * SHARDS + t]]
+        return 0
+
+    lax.fori_loop(0, SHARDS, pick_lent, 0)
     pl.semaphore_wait(barrier, SHARDS)
-
-    def adapter_swap():
-        return pltpu.make_async_remote_copy(
-            adp_ref, all_adp.at[pl.ds(grp * slot_count, slot_count)], xa_send, xa_recv,
-            device_id=(1 - grp, me), device_id_type=MESH)
-
-    adapter_swap().start()
+    each_peer(lambda t: lend(t).start())
+    lend(me).start()
 
     def send_w(p, y, h, kind):
         s = p * 4 + y * 2 + core
@@ -77,10 +92,13 @@
     def take_w(s, h):
         pltpu.make_async_copy(wbuf.at[s, h], wbuf.at[s, h], w_recv.at[s * 2 + h]).wait()
 
-    def with_plane(k, do):
-        d = (k + 1) // 2
-        p = plane + d * (2 * (k % 2) - 1)
-        pl.when((k >= 0) & (k < 2 * PLANES - 1) & (p >= 0) & (p < PLANES))(functools.partial(do, p))
+    def with_planes(d, do):
+        for sign in (-1, 1):
+            p = plane + sign * d
+            ok = (d >= 0) & (p >= 0) & (p < PLANES)
+            if sign > 0:
+                ok = ok & (d > 0)
+            pl.when(ok)(functools.partial(do, p))
 
     def along_planes(p, h, act):
         @pl.when((p <= plane) & (plane < PLANES - 1))
@@ -162,26 +180,24 @@
             gbuf.at[grp * SHARDS + k], gbuf.at[grp * SHARDS + k], xg_send.at[k], xg_recv.at[k],
             device_id=(1 - grp, me), device_id_type=MESH)
 
-    def each_peer(do):
-        def one(p, _):
-            do((me + p) % SHARDS)
-            return 0
-        lax.fori_loop(1, SHARDS, one, 0)
-
     def pick():
-        keep.wait()
-        adapter_swap().wait_recv()
-
-        def one(t, _):
-            picked[t] = all_adp[slots_ref[grp * SHARDS + t]]
-            return 0
-
-        lax.fori_loop(0, SHARDS, one, 0)
-        each_peer(lambda k: send_piece(k).start())
+        def choose(t):
+            lend(t).wait_recv()
+            tile = grp * SHARDS + t
+            picked[t] = jnp.where(owned_ref[tile] == 1, adp_ref[local_ref[tile]], borrowed[t])
+
+        def one(t):
+            choose(t)
+            send_piece(t).start()
+
+        each_peer(one)
+        choose(me)
         pieces[me] = picked[me]
 
     def adapt():
-        each_peer(lambda k: pltpu.make_async_copy(pieces.at[k], pieces.at[k], a_recv.at[k]).wait())
+        tok_copy.wait()
+        cot_copy.wait()
+        each_peer(lambda k: pltpu.make_async_copy(pieces.at[k], pieces.at[k], a_recv.at[k]).wait(), -1)
         pair = 2 * piece_cols
         for m in range(SHARDS // 2):
             down_t[:, m * pair:(m + 1) * pair] = jnp.concatenate([pieces[2 * m], pieces[2 * m + 1]], axis=1)
@@ -217,35 +233,41 @@
         def one(k):
             pltpu.make_async_copy(gbuf.at[grp * SHARDS + k], gbuf.at[grp * SHARDS + k], g_recv.at[k]).wait()
             swap_term(k).start()
-        each_peer(one)
-
-    lags = (0, 1, 2, 3, 5)
+        each_peer(one, -1)
 
     def turn(j, _):
-        with_plane(j - lags[0], plane_step)
-        with_plane(j - lags[1], row_step)
-        with_plane(j - lags[2], group_step)
-        with_plane(j - lags[3], core_step)
-        pl.when(j == 2)(pick)
-        pl.when(j == 4)(adapt)
-        pl.when(j == 6)(hand_on)
-        with_plane(j - lags[4], compute_step)
-        return 0
-
-    lax.fori_loop(0, 2 * PLANES - 1 + lags[4], turn, 0)
+        with_planes(j, plane_step)
+        pl.when(j == 0)(pick)
+        with_planes(j - 1, group_step)
+        with_planes(j, row_step)
+        with_planes(j - 1, core_step)
+        pl.when(j == 1)(adapt)
+        with_planes(j - 2, compute_step)
+        return 0
+
+    lax.fori_loop(0, PLANES, turn, 0)
+
+    def tail(d, _):
+        pl.when(d == PLANES - 1)(lambda: with_planes(d, group_step))
+        pl.when(d == PLANES - 1)(lambda: with_planes(d, core_step))
+        pl.when(d == PLANES - 1)(hand_on)
+        with_planes(d, compute_step)
+        return 0
+
+    lax.fori_loop(PLANES - 2, PLANES, tail, 0)
     keys_ref[...] = acc[...].astype(jnp.bfloat16)
 
-    def drain(k, _):
-        with_plane(k, drain_step)
-        return 0
-
-    lax.fori_loop(0, 2 * PLANES - 1, drain, 0)
-    adapter_swap().wait_send()
+    def drain(d, _):
+        with_planes(d, drain_step)
+        return 0
+
+    lax.fori_loop(0, PLANES, drain, 0)
     each_peer(lambda k: send_piece(k).wait_send())
     each_peer(lambda k: send_term(k).wait_send())
 
     def swapped(k, _):
         other = gbuf.at[(1 - grp) * SHARDS + k]
+        lend(k).wait_send()
         swap_term(k).wait_send()
         pltpu.make_async_copy(other, other, xg_recv.at[k]).wait()
         return 0
@@ -279,7 +301,11 @@
     key_columns = cotangent.shape[1]
     shard_rows = frozen_weight.shape[0]
     halves = frozen_weight.reshape(2, shard_rows // 2, key_columns)
+    local = slots - lax.axis_index("grp") * slot_count
+    near = jnp.clip(local, 0, slot_count - 1)
+    owned = (local == near).astype(jnp.int32)
     vmem = pl.BlockSpec(memory_space=pltpu.VMEM)
+    place = pl.BlockSpec(memory_space=pl.ANY)
     smem = pl.BlockSpec(memory_space=pltpu.SMEM)
     bf16 = jnp.bfloat16
     dma = pltpu.SemaphoreType.DMA
@@ -290,25 +316,28 @@
             jax.ShapeDtypeStruct((rows, width), bf16),
             jax.ShapeDtypeStruct((tiles, rank, piece_cols), bf16),
         ),
-        in_specs=[smem, vmem, vmem, pl.BlockSpec(memory_space=pl.ANY), vmem],
+        in_specs=[smem, smem, place, place, place, place],
         out_specs=(vmem, vmem, vmem),
         scratch_shapes=[
+            pltpu.VMEM(tokens.shape, bf16),
+            pltpu.VMEM(cotangent.shape, bf16),
+            pltpu.VMEM(adapters_t.shape, bf16),
             pltpu.VMEM((SHARDS, 2, shard_rows // 2, key_columns), bf16),
-            pltpu.VMEM((tiles, rank, piece_cols), bf16),
+            pltpu.VMEM((SHARDS, rank, piece_cols), bf16),
+            pltpu.VMEM((SHARDS, rank, piece_cols), bf16),
             pltpu.VMEM((SHARDS, rank, piece_cols), bf16),
             pltpu.VMEM((SHARDS, rank, piece_cols), bf16),
             pltpu.VMEM((rank, SHARDS * piece_cols), bf16),
             pltpu.VMEM((SHARDS, rank, piece_cols), bf16),
             pltpu.VMEM((rows, key_columns), jnp.float32),
             pltpu.VMEM((rows, rank), bf16),
-            dma((SHARDS * 5,)), dma((2 * SHARDS,)), dma, dma, dma,
+            dma((SHARDS * 5,)), dma((2 * SHARDS,)), dma((3,)), dma((SHARDS,)), dma((SHARDS,)),
             dma((SHARDS,)), dma((SHARDS,)), dma((SHARDS,)), dma((SHARDS,)), dma((SHARDS,)), dma((SHARDS,)),
         ],
         compiler_params=pltpu.CompilerParams(
             collective_id=0, has_side_effects=True, vmem_limit_bytes=50 * 1024 * 1024),
         name="exchange",
-    )(slots, tokens, cotangent, halves, adapters_t)
-    local = slots - lax.axis_index("grp") * slot_count
+    )(near, owned, tokens, cotangent, halves, adapters_t)
     grads = pl.pallas_call(
         sum_kernel,
         out_shape=jax.ShapeDtypeStruct((slot_count, rank, piece_cols), jnp.float32),

time: 183 us -> 188 us (1.027)
  Pallas kernels: 174 us -> 178 us
    pallas_call x1, Pallas kernels: 171 us -> 175 us  [on_block(): pl.pallas_call(exchange_kernel, out_shape=(jax.ShapeDtypeStruct((rows, ke...]
where the time goes in v2:
time: 188 us; the launch traced here: 187 us
  Pallas kernels  178 us (95%)
  local copies, waits for them, and re-layouts  7.24 us (4%)
    pallas_call x1, Pallas kernels, on_block(): pl.pallas_call(exchange_kernel, out_shape=(jax.ShapeDtypeStruct((rows, ke...  175 us
    unnamed x12, local copies, waits for them, and re-layouts  7.24 us

profile of v2, /device:TPU:0, one launch (start us, length us, event | category | flops | bytes accessed | tf_op | source)
XLA Modules:
  0.0 186.9 jit_solution(9433344574039912375)
XLA Ops:
  0.6 0.9 select_reduce_fusion
  1.5 0.0 copy-start.1
  1.5 1.3 copy-done.1
  2.8 0.0 copy-start.2
  2.8 1.2 copy-done.2
  4.1 0.0 copy-start.3
  4.1 0.9 copy-done.3
  5.0 175.3 %exchange.1 = (bf16[128,1024]{1,0:T(8,128)(2,1)S(1)}, bf16[128,8192]{1,0:T(8,128)(2,1)}, bf16[32,64,576]{2,1,0:T(8,128)(2,1)}) custom-call(s32[32]{0:T(128)S(1)} %broadcast_clamp_fusion.local_ref, s32[32]{0:T(128)S(1)} %get-tuple-element.9.owned_ref, bf16[128,8192]{1,0:T(8,128)(2,1)} %tok_hbm.1, bf16[128,1024]{1,0:T(8,128)(2,1)S(1)} %copy-done.3, ...), custom_call_target="tpu_custom_call" | custom-call | tf_op jit(solution)/shard_map/exchange/pallas_call | solution.py:312
  180.3 0.0 copy-start
  180.3 1.7 copy-done
  182.0 0.0 copy-start.4
  182.0 2.9 %slot_sums.1 = f32[16,64,576]{2,1,0:T(8,128)} custom-call(s32[32]{0:T(128)S(1)} %get-tuple-element.10.local_ref, bf16[32,64,576]{2,1,0:T(8,128)(2,1)S(1)} %copy-done), custom_call_target="tpu_custom_call" | custom-call | tf_op jit(solution)/shard_map/slot_sums/pallas_call | solution.py:341
  184.9 0.7 copy.11
  185.6 0.0 copy-done.4
  185.6 1.3 copy.12
  (2 shorter events, 0.0 us)
Async XLA Ops:
  1.5 1.3 copy-start.1
  2.8 1.2 copy-start.2
  4.1 0.9 copy-start.3
  180.3 1.7 copy-start
  182.0 3.6 %copy-start.4 = (bf16[128,8192]{1,0:T(8,128)(2,1)S(1)}, bf16[128,8192]{1,0:T(8,128)(2,1)}, u32[]{:S(2)}) copy-start(bf16[128,8192]{1,0:T(8,128)(2,1)} %get-tuple-element.15) | copy-start | bytes 6291460

commit v3 on v2

--- a/solution.py
+++ b/solution.py
@@ -28,7 +28,7 @@
     local_ref, owned_ref, tok_hbm, cot_hbm, w_ref, adp_hbm,
     keys_ref, tg_ref, gbuf,
     tok_ref, cot_ref, adp_ref,
-    wbuf, lent, borrowed, picked, pieces, down_t, gsend, acc, back,
+    wbuf, lent, borrowed, picked, pieces, down_t, gsend, acc, back, cot_t,
     w_send, w_recv, own_sem, xa_send, xa_recv, a_send, a_recv, g_send, g_recv, xg_send, xg_recv,
 ):
     grp = lax.axis_index("grp")
@@ -159,7 +159,7 @@
             cols = pl.ds(pl.multiple_of(s * shard_rows, shard_rows), shard_rows)
             block = wbuf[s].reshape(shard_rows, cot_ref.shape[1])
             acc[...] += dot(tok_ref[:, cols], block)
-            grad = nt_dot(cot_ref[...], block) + adapter_scale * dot(back[...], down_t[:, cols])
+            grad = dot(block, cot_t[...]).T + adapter_scale * dot(back[...], down_t[:, cols])
             tg_ref[:, cols] = grad.astype(jnp.bfloat16)
             return 0
 
@@ -203,17 +203,17 @@
             down_t[:, m * pair:(m + 1) * pair] = jnp.concatenate([pieces[2 * m], pieces[2 * m + 1]], axis=1)
         up = down_t[:, width:]
         hidden = jnp.zeros((TILE_ROWS, rank), jnp.float32)
-        hidden_t = jnp.zeros((rank, TILE_ROWS), jnp.float32)
         step = width // 4
         for q in range(4):
             t_cols = tok_ref[:, q * step:(q + 1) * step]
             d_cols = down_t[:, q * step:(q + 1) * step]
             hidden = hidden + nt_dot(t_cols, d_cols)
-            hidden_t = hidden_t + nt_dot(d_cols, t_cols)
+        hidden_t = hidden.T.astype(jnp.bfloat16)
         hidden = hidden.astype(jnp.bfloat16)
-        hidden_t = hidden_t.astype(jnp.bfloat16)
-        back[...] = nt_dot(cot_ref[...], up).astype(jnp.bfloat16)
-        back_t = nt_dot(up, cot_ref[...]).astype(jnp.bfloat16)
+        back_wide = nt_dot(cot_ref[...], up)
+        back[...] = back_wide.astype(jnp.bfloat16)
+        back_t = back_wide.T.astype(jnp.bfloat16)
+        cot_t[...] = cot_ref[...].T
         acc[...] = adapter_scale * dot(hidden, up)
         for m in range(SHARDS // 2):
             first, last = m * pair, (m + 1) * pair
@@ -331,6 +331,7 @@
             pltpu.VMEM((SHARDS, rank, piece_cols), bf16),
             pltpu.VMEM((rows, key_columns), jnp.float32),
             pltpu.VMEM((rows, rank), bf16),
+            pltpu.VMEM((key_columns, rows), bf16),
             dma((SHARDS * 5,)), dma((2 * SHARDS,)), dma((3,)), dma((SHARDS,)), dma((SHARDS,)),
             dma((SHARDS,)), dma((SHARDS,)), dma((SHARDS,)), dma((SHARDS,)), dma((SHARDS,)), dma((SHARDS,)),
         ],

time: 188 us -> 188 us (level)
  no operation moved by 1% of the time
where the time goes in v3:
time: 188 us; the launch traced here: 187 us
  Pallas kernels  178 us (95%)
  local copies, waits for them, and re-layouts  7.24 us (4%)
    pallas_call x1, Pallas kernels, on_block(): pl.pallas_call(exchange_kernel, out_shape=(jax.ShapeDtypeStruct((rows, ke...  175 us
    unnamed x12, local copies, waits for them, and re-layouts  7.24 us

profile of v3, /device:TPU:0, one launch (start us, length us, event | category | flops | bytes accessed | tf_op | source)
XLA Modules:
  0.0 186.9 jit_solution(15165244836335144683)
XLA Ops:
  0.6 0.9 select_reduce_fusion
  1.5 0.0 copy-start.1
  1.5 1.3 copy-done.1
  2.8 0.0 copy-start.2
  2.8 1.2 copy-done.2
  4.1 0.0 copy-start.3
  4.1 0.9 copy-done.3
  5.0 175.3 %exchange.1 = (bf16[128,1024]{1,0:T(8,128)(2,1)S(1)}, bf16[128,8192]{1,0:T(8,128)(2,1)}, bf16[32,64,576]{2,1,0:T(8,128)(2,1)}) custom-call(s32[32]{0:T(128)S(1)} %broadcast_clamp_fusion.local_ref, s32[32]{0:T(128)S(1)} %get-tuple-element.9.owned_ref, bf16[128,8192]{1,0:T(8,128)(2,1)} %tok_hbm.1, bf16[128,1024]{1,0:T(8,128)(2,1)S(1)} %copy-done.3, ...), custom_call_target="tpu_custom_call" | custom-call | tf_op jit(solution)/shard_map/exchange/pallas_call | solution.py:312
  180.3 0.0 copy-start
  180.3 1.7 copy-done
  182.0 0.0 copy-start.4
  182.0 2.9 %slot_sums.1 = f32[16,64,576]{2,1,0:T(8,128)} custom-call(s32[32]{0:T(128)S(1)} %get-tuple-element.10.local_ref, bf16[32,64,576]{2,1,0:T(8,128)(2,1)S(1)} %copy-done), custom_call_target="tpu_custom_call" | custom-call | tf_op jit(solution)/shard_map/slot_sums/pallas_call | solution.py:342
  184.9 0.7 copy.11
  185.6 0.0 copy-done.4
  185.6 1.3 copy.12
  (2 shorter events, 0.0 us)
Async XLA Ops:
  1.5 1.3 copy-start.1
  2.8 1.2 copy-start.2
  4.1 0.9 copy-start.3
  180.3 1.7 copy-start
  182.0 3.6 %copy-start.4 = (bf16[128,8192]{1,0:T(8,128)(2,1)S(1)}, bf16[128,8192]{1,0:T(8,128)(2,1)}, u32[]{:S(2)}) copy-start(bf16[128,8192]{1,0:T(8,128)(2,1)} %get-tuple-element.15) | copy-start | bytes 6291460

commit v4 on v3

--- a/solution.py
+++ b/solution.py
@@ -115,25 +115,47 @@
     def finish(copy):
         copy.wait_send()
 
+    def from_plane(p, act):
+        along_planes(p, grp, act)
+        act(send_w(p, row, grp, 2))
+        pl.when(p != plane)(lambda: act(send_w(p, row, grp, 3)))
+        act(send_w(p, row, grp, 4))
+        pl.when(p == plane)(lambda: act(send_w(p, row, 1 - grp, 4)))
+
+    def from_group(p, act):
+        @pl.when(p != plane)
+        def _():
+            act(send_w(p, row, 1 - grp, 2))
+            act(send_w(p, row, 1 - grp, 4))
+
+        @pl.when(p == plane)
+        def _():
+            act(send_w(p, 1 - row, 1 - grp, 4))
+
+    def from_row(p, act):
+        pl.when(p == plane)(lambda: act(send_w(p, 1 - row, grp, 3)))
+        act(send_w(p, 1 - row, grp, 4))
+
+    def from_corner(p, act):
+        pl.when(p != plane)(lambda: act(send_w(p, 1 - row, 1 - grp, 4)))
+
     def plane_step(p):
-        for h in range(2):
-            take_w(p * 4 + row * 2 + core, h)
-            along_planes(p, h, start)
-
-            @pl.when(grp == h)
-            def _():
-                send_w(p, row, h, 2).start()
-
-            send_w(p, row, h, 4).start()
+        take_w(p * 4 + row * 2 + core, grp)
+        pl.when(p == plane)(lambda: take_w(p * 4 + row * 2 + core, 1 - grp))
+        from_plane(p, start)
+
+    def group_step(p):
+        pl.when(p != plane)(lambda: take_w(p * 4 + row * 2 + core, 1 - grp))
+        pl.when(p == plane)(lambda: take_w(p * 4 + (1 - row) * 2 + core, 1 - grp))
+        from_group(p, start)
 
     def row_step(p):
         take_w(p * 4 + (1 - row) * 2 + core, grp)
-        send_w(p, 1 - row, grp, 3).start()
-        send_w(p, 1 - row, grp, 4).start()
-
-    def group_step(p):
-        take_w(p * 4 + (1 - row) * 2 + core, 1 - grp)
-        send_w(p, 1 - row, 1 - grp, 4).start()
+        from_row(p, start)
+
+    def corner_step(p):
+        pl.when(p != plane)(lambda: take_w(p * 4 + (1 - row) * 2 + core, 1 - grp))
+        from_corner(p, start)
 
     def core_step(p):
         for y in range(2):
@@ -141,17 +163,8 @@
                 take_w(p * 4 + y * 2 + 1 - core, h)
 
     def drain_step(p):
-        for h in range(2):
-            along_planes(p, h, finish)
-
-            @pl.when(grp == h)
-            def _():
-                send_w(p, row, h, 2).wait_send()
-
-            send_w(p, row, h, 4).wait_send()
-        send_w(p, 1 - row, grp, 3).wait_send()
-        send_w(p, 1 - row, grp, 4).wait_send()
-        send_w(p, 1 - row, 1 - grp, 4).wait_send()
+        for leaves in (from_plane, from_group, from_row, from_corner):
+            leaves(p, finish)
 
     def compute_step(p):
         def shard(i, _):
@@ -238,23 +251,16 @@
     def turn(j, _):
         with_planes(j, plane_step)
         pl.when(j == 0)(pick)
+        with_planes(j - 1, row_step)
         with_planes(j - 1, group_step)
-        with_planes(j, row_step)
-        with_planes(j - 1, core_step)
         pl.when(j == 1)(adapt)
+        with_planes(j - 2, corner_step)
+        with_planes(j - 2, core_step)
         with_planes(j - 2, compute_step)
-        return 0
-
-    lax.fori_loop(0, PLANES, turn, 0)
-
-    def tail(d, _):
-        pl.when(d == PLANES - 1)(lambda: with_planes(d, group_step))
-        pl.when(d == PLANES - 1)(lambda: with_planes(d, core_step))
-        pl.when(d == PLANES - 1)(hand_on)
-        with_planes(d, compute_step)
-        return 0
-
-    lax.fori_loop(PLANES - 2, PLANES, tail, 0)
+        pl.when(j == PLANES)(hand_on)
+        return 0
+
+    lax.fori_loop(0, PLANES + 2, turn, 0)
     keys_ref[...] = acc[...].astype(jnp.bfloat16)
 
     def drain(d, _):

time: 188 us -> 179 us (0.952)
  the two profiles are of different devices: /device:TPU:0 before, /device:TPU:21 now
where the time goes in v4:
time: 179 us
  Pallas kernels  170 us (95%)
  local copies, waits for them, and re-layouts  7.24 us (4%)
    pallas_call x1, Pallas kernels, on_block(): pl.pallas_call(exchange_kernel, out_shape=(jax.ShapeDtypeStruct((rows, ke...  167 us
    unnamed x12, local copies, waits for them, and re-layouts  7.24 us

profile of v4, /device:TPU:21, one launch (start us, length us, event | category | flops | bytes accessed | tf_op | source)
XLA Modules:
  0.0 179.1 jit_solution(6031870444731225032)
XLA Ops:
  0.6 0.9 select_reduce_fusion
  1.5 0.0 copy-start.1
  1.5 1.3 copy-done.1
  2.8 0.0 copy-start.2
  2.8 1.2 copy-done.2
  4.1 0.0 copy-start.3
  4.1 0.9 copy-done.3
  5.0 167.4 %exchange.1 = (bf16[128,1024]{1,0:T(8,128)(2,1)S(1)}, bf16[128,8192]{1,0:T(8,128)(2,1)}, bf16[32,64,576]{2,1,0:T(8,128)(2,1)}) custom-call(s32[32]{0:T(128)S(1)} %broadcast_clamp_fusion.local_ref, s32[32]{0:T(128)S(1)} %get-tuple-element.9.owned_ref, bf16[128,8192]{1,0:T(8,128)(2,1)} %tok_hbm.1, bf16[128,1024]{1,0:T(8,128)(2,1)S(1)} %copy-done.3, ...), custom_call_target="tpu_custom_call" | custom-call | tf_op jit(solution)/shard_map/exchange/pallas_call | solution.py:318
  172.4 0.0 copy-start
  172.4 1.7 copy-done
  174.2 0.0 copy-start.4
  174.2 2.9 %slot_sums.1 = f32[16,64,576]{2,1,0:T(8,128)} custom-call(s32[32]{0:T(128)S(1)} %get-tuple-element.10.local_ref, bf16[32,64,576]{2,1,0:T(8,128)(2,1)S(1)} %copy-done), custom_call_target="tpu_custom_call" | custom-call | tf_op jit(solution)/shard_map/slot_sums/pallas_call | solution.py:348
  177.0 0.7 copy.11
  177.7 0.0 copy-done.4
  177.7 1.3 copy.12
  (2 shorter events, 0.0 us)
Async XLA Ops:
  1.5 1.3 copy-start.1
  2.8 1.2 copy-start.2
  4.1 0.9 copy-start.3
  172.4 1.7 copy-start
  174.2 3.6 %copy-start.4 = (bf16[128,8192]{1,0:T(8,128)(2,1)S(1)}, bf16[128,8192]{1,0:T(8,128)(2,1)}, u32[]{:S(2)}) copy-start(bf16[128,8192]{1,0:T(8,128)(2,1)} %get-tuple-element.15) | copy-start | bytes 6291460

commit v5 on v4

--- a/solution.py
+++ b/solution.py
@@ -68,9 +68,12 @@
             device_id=(1 - grp, me), device_id_type=MESH)
 
     def pick_lent(t, _):
-        lent[t] = adp_ref[local_ref[(1 - grp) * SHARDS + t]]
-        return 0
-
+        lent[t, :, :piece_cols] = adp_ref[local_ref[(1 - grp) * SHARDS + t]]
+        return 0
+
+    edge = piece_cols // 128 * 128
+    for buf in (lent, picked, gsend):
+        buf[:, :, edge:] = jnp.zeros_like(buf[:, :, edge:])
     lax.fori_loop(0, SHARDS, pick_lent, 0)
     pl.semaphore_wait(barrier, SHARDS)
     each_peer(lambda t: lend(t).start())
@@ -197,7 +200,8 @@
         def choose(t):
             lend(t).wait_recv()
             tile = grp * SHARDS + t
-            picked[t] = jnp.where(owned_ref[tile] == 1, adp_ref[local_ref[tile]], borrowed[t])
+            picked[t, :, :piece_cols] = jnp.where(
+                owned_ref[tile] == 1, adp_ref[local_ref[tile]], borrowed[t, :, :piece_cols])
 
         def one(t):
             choose(t)
@@ -213,7 +217,8 @@
         each_peer(lambda k: pltpu.make_async_copy(pieces.at[k], pieces.at[k], a_recv.at[k]).wait(), -1)
         pair = 2 * piece_cols
         for m in range(SHARDS // 2):
-            down_t[:, m * pair:(m + 1) * pair] = jnp.concatenate([pieces[2 * m], pieces[2 * m + 1]], axis=1)
+            down_t[:, m * pair:(m + 1) * pair] = jnp.concatenate(
+                [pieces[2 * m, :, :piece_cols], pieces[2 * m + 1, :, :piece_cols]], axis=1)
         up = down_t[:, width:]
         hidden = jnp.zeros((TILE_ROWS, rank), jnp.float32)
         step = width // 4
@@ -236,8 +241,8 @@
                 term = jnp.concatenate(
                     [dot(back_t, tok_ref[:, first:width]), dot(hidden_t, cot_ref[:, :last - width])], axis=1)
             term = adapter_scale * term
-            gsend[2 * m] = term[:, :piece_cols].astype(jnp.bfloat16)
-            gsend[2 * m + 1] = term[:, piece_cols:].astype(jnp.bfloat16)
+            gsend[2 * m, :, :piece_cols] = term[:, :piece_cols].astype(jnp.bfloat16)
+            gsend[2 * m + 1, :, :piece_cols] = term[:, piece_cols:].astype(jnp.bfloat16)
         each_peer(lambda k: send_term(k).start())
         gbuf[grp * SHARDS + me] = gsend[me]
         swap_term(me).start()
@@ -256,8 +261,8 @@
         pl.when(j == 1)(adapt)
         with_planes(j - 2, corner_step)
         with_planes(j - 2, core_step)
+        pl.when(j == PLANES - 1)(hand_on)
         with_planes(j - 2, compute_step)
-        pl.when(j == PLANES)(hand_on)
         return 0
 
     lax.fori_loop(0, PLANES + 2, turn, 0)
@@ -290,7 +295,7 @@
 
         @pl.when((slot >= 0) & (slot < slot_count))
         def _():
-            out_ref[slot] += term_ref[t].astype(jnp.float32)
+            out_ref[slot] += term_ref[t, :, :out_ref.shape[2]].astype(jnp.float32)
 
         return 0
 
@@ -303,6 +308,7 @@
     adapters_t = jnp.swapaxes(adapters, 1, 2)
     slot_count, rank, piece_cols = adapters_t.shape
     tiles = slots.shape[0]
+    wide = -(-piece_cols // 128) * 128
     rows, width = tokens.shape
     key_columns = cotangent.shape[1]
     shard_rows = frozen_weight.shape[0]
@@ -320,7 +326,7 @@
         out_shape=(
             jax.ShapeDtypeStruct((rows, key_columns), bf16),
             jax.ShapeDtypeStruct((rows, width), bf16),
-            jax.ShapeDtypeStruct((tiles, rank, piece_cols), bf16),
+            jax.ShapeDtypeStruct((tiles, rank, wide), bf16),
         ),
         in_specs=[smem, smem, place, place, place, place],
         out_specs=(vmem, vmem, vmem),
@@ -329,12 +335,12 @@
             pltpu.VMEM(cotangent.shape, bf16),
             pltpu.VMEM(adapters_t.shape, bf16),
             pltpu.VMEM((SHARDS, 2, shard_rows // 2, key_columns), bf16),
-            pltpu.VMEM((SHARDS, rank, piece_cols), bf16),
-            pltpu.VMEM((SHARDS, rank, piece_cols), bf16),
-            pltpu.VMEM((SHARDS, rank, piece_cols), bf16),
-            pltpu.VMEM((SHARDS, rank, piece_cols), bf16),
+            pltpu.VMEM((SHARDS, rank, wide), bf16),
+            pltpu.VMEM((SHARDS, rank, wide), bf16),
+            pltpu.VMEM((SHARDS, rank, wide), bf16),
+            pltpu.VMEM((SHARDS, rank, wide), bf16),
             pltpu.VMEM((rank, SHARDS * piece_cols), bf16),
-            pltpu.VMEM((SHARDS, rank, piece_cols), bf16),
+            pltpu.VMEM((SHARDS, rank, wide), bf16),
             pltpu.VMEM((rows, key_columns), jnp.float32),
             pltpu.VMEM((rows, rank), bf16),
             pltpu.VMEM((key_columns, rows), bf16),
@@ -342,7 +348,7 @@
             dma((SHARDS,)), dma((SHARDS,)), dma((SHARDS,)), dma((SHARDS,)), dma((SHARDS,)), dma((SHARDS,)),
         ],
         compiler_params=pltpu.CompilerParams(
-            collective_id=0, has_side_effects=True, vmem_limit_bytes=50 * 1024 * 1024),
+            collective_id=0, has_side_effects=True, vmem_limit_bytes=60 * 1024 * 1024),
         name="exchange",
     )(near, owned, tokens, cotangent, halves, adapters_t)
     grads = pl.pallas_call(

time: 179 us -> 163 us (0.911)
  Pallas kernels: 170 us -> 157 us
  local copies, waits for them, and re-layouts: 7.24 us -> 3.76 us
    pallas_call x1, Pallas kernels: 167 us -> 154 us  [on_block(): pl.pallas_call(exchange_kernel, out_shape=(jax.ShapeDtypeStruct((rows, ke...]
    unnamed x12 -> x8, local copies, waits for them, and re-layouts: 7.24 us -> 3.76 us
where the time goes in v5:
time: 163 us
  Pallas kernels  157 us (96%)
  local copies, waits for them, and re-layouts  3.76 us (2%)
  other arithmetic  1.89 us (1%)
    pallas_call x1, Pallas kernels, on_block(): pl.pallas_call(exchange_kernel, out_shape=(jax.ShapeDtypeStruct((rows, ke...  154 us
    unnamed x8, local copies, waits for them, and re-layouts  3.76 us

profile of v5, /device:TPU:21, one launch (start us, length us, event | category | flops | bytes accessed | tf_op | source)
XLA Modules:
  0.0 162.9 jit_solution(10505094277103255480)
XLA Ops:
  0.6 0.9 select_reduce_fusion
  1.5 0.5 compare_convert_fusion
  2.0 0.5 broadcast_clamp_fusion.local_ref
  2.5 153.8 %exchange.1 = (bf16[128,1024]{1,0:T(8,128)(2,1)}, bf16[128,8192]{1,0:T(8,128)(2,1)}, bf16[32,64,640]{2,1,0:T(8,128)(2,1)}) custom-call(s32[32]{0:T(128)} %broadcast_clamp_fusion.local_ref, s32[32]{0:T(128)} %get-tuple-element.9.owned_ref, bf16[128,8192]{1,0:T(8,128)(2,1)} %tok_hbm.1, bf16[128,1024]{1,0:T(8,128)(2,1)} %cot_hbm.1, ...), custom_call_target="tpu_custom_call" | custom-call | tf_op jit(solution)/shard_map/exchange/pallas_call | solution.py:324
  156.3 0.0 copy-start
  156.3 1.7 %copy-done = bf16[32,64,640]{2,1,0:T(8,128)(2,1)S(1)} copy-done((bf16[32,64,640]{2,1,0:T(8,128)(2,1)S(1)}, bf16[32,64,640]{2,1,0:T(8,128)(2,1)}, u32[]{:S(2)}) %copy-start) | copy-done | bytes 2621464
  158.0 0.0 copy-start.2
  158.0 0.0 copy-start.1
  158.0 2.9 %slot_sums.1 = f32[16,64,576]{2,1,0:T(8,128)} custom-call(s32[32]{0:T(128)S(1)} %get-tuple-element.10.local_ref, bf16[32,64,640]{2,1,0:T(8,128)(2,1)S(1)} %copy-done), custom_call_target="tpu_custom_call" | custom-call | tf_op jit(solution)/shard_map/slot_sums/pallas_call | solution.py:354
  160.9 0.0 copy-done.2
  160.9 0.7 copy.11
  161.6 0.0 copy-done.1
  161.6 1.3 copy.12
Async XLA Ops:
  156.3 1.7 %copy-start = (bf16[32,64,640]{2,1,0:T(8,128)(2,1)S(1)}, bf16[32,64,640]{2,1,0:T(8,128)(2,1)}, u32[]{:S(2)}) copy-start(bf16[32,64,640]{2,1,0:T(8,128)(2,1)} %get-tuple-element.8.term_ref) | copy-start | bytes 7864324
  158.0 2.9 %copy-start.2 = (bf16[128,1024]{1,0:T(8,128)(2,1)S(1)}, bf16[128,1024]{1,0:T(8,128)(2,1)}, u32[]{:S(2)}) copy-start(bf16[128,1024]{1,0:T(8,128)(2,1)} %get-tuple-element.14) | copy-start | bytes 786436
  158.0 3.6 %copy-start.1 = (bf16[128,8192]{1,0:T(8,128)(2,1)S(1)}, bf16[128,8192]{1,0:T(8,128)(2,1)}, u32[]{:S(2)}) copy-start(bf16[128,8192]{1,0:T(8,128)(2,1)} %get-tuple-element.15) | copy-start | bytes 6291460

commit v6 on v5

--- a/solution.py
+++ b/solution.py
@@ -56,11 +56,11 @@
     pl.semaphore_signal(barrier, inc=1, device_id=(1 - grp, me), device_id_type=MESH)
     adp_copy.wait()
 
-    def each_peer(do, away=1):
+    def each_peer(do, away=1, first=1, last=SHARDS):
         def one(p, _):
             do((me + away * p) % SHARDS)
             return 0
-        lax.fori_loop(1, SHARDS, one, 0)
+        lax.fori_loop(first, last, one, 0)
 
     def lend(t):
         return pltpu.make_async_remote_copy(
@@ -118,38 +118,42 @@
     def finish(copy):
         copy.wait_send()
 
+    def whole(p):
+        return (p == plane) | (core == 0)
+
     def from_plane(p, act):
         along_planes(p, grp, act)
+        pl.when(core == 0)(lambda: along_planes(p, 1 - grp, act))
         act(send_w(p, row, grp, 2))
-        pl.when(p != plane)(lambda: act(send_w(p, row, grp, 3)))
+        pl.when(~whole(p))(lambda: act(send_w(p, row, grp, 3)))
         act(send_w(p, row, grp, 4))
-        pl.when(p == plane)(lambda: act(send_w(p, row, 1 - grp, 4)))
+        pl.when(whole(p))(lambda: act(send_w(p, row, 1 - grp, 4)))
 
     def from_group(p, act):
-        @pl.when(p != plane)
+        @pl.when(~whole(p))
         def _():
             act(send_w(p, row, 1 - grp, 2))
             act(send_w(p, row, 1 - grp, 4))
 
-        @pl.when(p == plane)
+        @pl.when(whole(p))
         def _():
             act(send_w(p, 1 - row, 1 - grp, 4))
 
     def from_row(p, act):
-        pl.when(p == plane)(lambda: act(send_w(p, 1 - row, grp, 3)))
+        pl.when(whole(p))(lambda: act(send_w(p, 1 - row, grp, 3)))
         act(send_w(p, 1 - row, grp, 4))
 
     def from_corner(p, act):
-        pl.when(p != plane)(lambda: act(send_w(p, 1 - row, 1 - grp, 4)))
+        pl.when(~whole(p))(lambda: act(send_w(p, 1 - row, 1 - grp, 4)))
 
     def plane_step(p):
         take_w(p * 4 + row * 2 + core, grp)
-        pl.when(p == plane)(lambda: take_w(p * 4 + row * 2 + core, 1 - grp))
+        pl.when(whole(p))(lambda: take_w(p * 4 + row * 2 + core, 1 - grp))
         from_plane(p, start)
 
     def group_step(p):
-        pl.when(p != plane)(lambda: take_w(p * 4 + row * 2 + core, 1 - grp))
-        pl.when(p == plane)(lambda: take_w(p * 4 + (1 - row) * 2 + core, 1 - grp))
+        pl.when(~whole(p))(lambda: take_w(p * 4 + row * 2 + core, 1 - grp))
+        pl.when(whole(p))(lambda: take_w(p * 4 + (1 - row) * 2 + core, 1 - grp))
         from_group(p, start)
 
     def row_step(p):
@@ -157,7 +161,7 @@
         from_row(p, start)
 
     def corner_step(p):
-        pl.when(p != plane)(lambda: take_w(p * 4 + (1 - row) * 2 + core, 1 - grp))
+        pl.when(~whole(p))(lambda: take_w(p * 4 + (1 - row) * 2 + core, 1 - grp))
         from_corner(p, start)
 
     def core_step(p):
@@ -196,7 +200,7 @@
             gbuf.at[grp * SHARDS + k], gbuf.at[grp * SHARDS + k], xg_send.at[k], xg_recv.at[k],
             device_id=(1 - grp, me), device_id_type=MESH)
 
-    def pick():
+    def pick(first, last):
         def choose(t):
             lend(t).wait_recv()
             tile = grp * SHARDS + t
@@ -207,9 +211,12 @@
             choose(t)
             send_piece(t).start()
 
-        each_peer(one)
-        choose(me)
-        pieces[me] = picked[me]
+        each_peer(one, 1, first, last)
+
+        @pl.when(last == SHARDS)
+        def _():
+            choose(me)
+            pieces[me] = picked[me]
 
     def adapt():
         tok_copy.wait()
@@ -247,21 +254,24 @@
         gbuf[grp * SHARDS + me] = gsend[me]
         swap_term(me).start()
 
-    def hand_on():
+    def hand_on(first, last):
         def one(k):
             pltpu.make_async_copy(gbuf.at[grp * SHARDS + k], gbuf.at[grp * SHARDS + k], g_recv.at[k]).wait()
             swap_term(k).start()
-        each_peer(one, -1)
+        each_peer(one, -1, first, last)
+
+    middle = SHARDS // 2
 
     def turn(j, _):
         with_planes(j, plane_step)
-        pl.when(j == 0)(pick)
         with_planes(j - 1, row_step)
+        pl.when(j < 2)(lambda: pick(1 + j * (middle - 1), middle + j * middle))
         with_planes(j - 1, group_step)
-        pl.when(j == 1)(adapt)
+        pl.when(j == 2)(adapt)
         with_planes(j - 2, corner_step)
         with_planes(j - 2, core_step)
-        pl.when(j == PLANES - 1)(hand_on)
+        pl.when((j == 3) | (j == 4))(
+            lambda: hand_on(1 + (j - 3) * (middle - 1), middle + (j - 3) * middle))
         with_planes(j - 2, compute_step)
         return 0
 

time: 163 us -> 155 us (0.951)
  the two profiles are of different devices: /device:TPU:21 before, /device:TPU:0 now
where the time goes in v6:
time: 155 us; the launch traced here: 154 us
  Pallas kernels  148 us (95%)
  local copies, waits for them, and re-layouts  3.76 us (2%)
  other arithmetic  1.89 us (1%)
    pallas_call x1, Pallas kernels, on_block(): pl.pallas_call(exchange_kernel, out_shape=(jax.ShapeDtypeStruct((rows, ke...  145 us
    unnamed x8, local copies, waits for them, and re-layouts  3.76 us

profile of v6, /device:TPU:0, one launch (start us, length us, event | category | flops | bytes accessed | tf_op | source)
XLA Modules:
  0.0 154.4 jit_solution(84366308193659960)
XLA Ops:
  0.6 0.9 select_reduce_fusion
  1.5 0.5 compare_convert_fusion
  2.0 0.5 broadcast_clamp_fusion.local_ref
  2.5 145.2 %exchange.1 = (bf16[128,1024]{1,0:T(8,128)(2,1)}, bf16[128,8192]{1,0:T(8,128)(2,1)}, bf16[32,64,640]{2,1,0:T(8,128)(2,1)}) custom-call(s32[32]{0:T(128)} %broadcast_clamp_fusion.local_ref, s32[32]{0:T(128)} %get-tuple-element.9.owned_ref, bf16[128,8192]{1,0:T(8,128)(2,1)} %tok_hbm.1, bf16[128,1024]{1,0:T(8,128)(2,1)} %cot_hbm.1, ...), custom_call_target="tpu_custom_call" | custom-call | tf_op jit(solution)/shard_map/exchange/pallas_call | solution.py:334
  147.7 0.0 copy-start
  147.8 1.7 %copy-done = bf16[32,64,640]{2,1,0:T(8,128)(2,1)S(1)} copy-done((bf16[32,64,640]{2,1,0:T(8,128)(2,1)S(1)}, bf16[32,64,640]{2,1,0:T(8,128)(2,1)}, u32[]{:S(2)}) %copy-start) | copy-done | bytes 2621464
  149.5 0.0 copy-start.2
  149.5 0.0 copy-start.1
  149.5 2.9 %slot_sums.1 = f32[16,64,576]{2,1,0:T(8,128)} custom-call(s32[32]{0:T(128)S(1)} %get-tuple-element.10.local_ref, bf16[32,64,640]{2,1,0:T(8,128)(2,1)S(1)} %copy-done), custom_call_target="tpu_custom_call" | custom-call | tf_op jit(solution)/shard_map/slot_sums/pallas_call | solution.py:364
  152.4 0.0 copy-done.2
  152.4 0.7 copy.11
  153.1 0.0 copy-done.1
  153.1 1.3 copy.12
Async XLA Ops:
  147.7 1.7 %copy-start = (bf16[32,64,640]{2,1,0:T(8,128)(2,1)S(1)}, bf16[32,64,640]{2,1,0:T(8,128)(2,1)}, u32[]{:S(2)}) copy-start(bf16[32,64,640]{2,1,0:T(8,128)(2,1)} %get-tuple-element.8.term_ref) | copy-start | bytes 7864324
  149.5 2.9 %copy-start.2 = (bf16[128,1024]{1,0:T(8,128)(2,1)S(1)}, bf16[128,1024]{1,0:T(8,128)(2,1)}, u32[]{:S(2)}) copy-start(bf16[128,1024]{1,0:T(8,128)(2,1)} %get-tuple-element.14) | copy-start | bytes 786436
  149.5 3.6 %copy-start.1 = (bf16[128,8192]{1,0:T(8,128)(2,1)S(1)}, bf16[128,8192]{1,0:T(8,128)(2,1)}, u32[]{:S(2)}) copy-start(bf16[128,8192]{1,0:T(8,128)(2,1)} %get-tuple-element.15) | copy-start | bytes 6291460

commit v7 on v6

--- a/solution.py
+++ b/solution.py
@@ -25,7 +25,7 @@
 
 
 def exchange_kernel(
-    local_ref, owned_ref, tok_hbm, cot_hbm, w_ref, adp_hbm,
+    slots_ref, tok_hbm, cot_hbm, w_ref, adp_hbm,
     keys_ref, tg_ref, gbuf,
     tok_ref, cot_ref, adp_ref,
     wbuf, lent, borrowed, picked, pieces, down_t, gsend, acc, back, cot_t,
@@ -36,7 +36,7 @@
     core = me % 2
     row = (me // 2) % 2
     plane = me // 4
-    rank, piece_cols = adp_ref.shape[1:]
+    slot_count, rank, piece_cols = adp_ref.shape
     width = tok_ref.shape[1]
     shard_rows = width // SHARDS
 
@@ -67,8 +67,13 @@
             lent.at[t], borrowed.at[t], xa_send.at[t], xa_recv.at[t],
             device_id=(1 - grp, me), device_id_type=MESH)
 
+    def local_of(tile):
+        local = slots_ref[tile] - grp * slot_count
+        held = jnp.minimum(jnp.maximum(local, 0), slot_count - 1)
+        return local == held, held
+
     def pick_lent(t, _):
-        lent[t, :, :piece_cols] = adp_ref[local_ref[(1 - grp) * SHARDS + t]]
+        lent[t, :, :piece_cols] = adp_ref[local_of((1 - grp) * SHARDS + t)[1]]
         return 0
 
     edge = piece_cols // 128 * 128
@@ -103,12 +108,12 @@
                 ok = ok & (d > 0)
             pl.when(ok)(functools.partial(do, p))
 
-    def along_planes(p, h, act):
-        @pl.when((p <= plane) & (plane < PLANES - 1))
+    def along_planes(p, h, act, reach=PLANES):
+        @pl.when((p <= plane) & (plane < PLANES - 1) & (plane + 1 - p <= reach))
         def _():
             act(send_w(p, row, h, 0))
 
-        @pl.when((p >= plane) & (plane > 0))
+        @pl.when((p >= plane) & (plane > 0) & (p - plane + 1 <= reach))
         def _():
             act(send_w(p, row, h, 1))
 
@@ -118,12 +123,14 @@
     def finish(copy):
         copy.wait_send()
 
+    near = PLANES - 2
+
     def whole(p):
-        return (p == plane) | (core == 0)
+        return (p == plane) | ((core == 0) & (p - plane <= near) & (plane - p <= near))
 
     def from_plane(p, act):
         along_planes(p, grp, act)
-        pl.when(core == 0)(lambda: along_planes(p, 1 - grp, act))
+        pl.when(core == 0)(lambda: along_planes(p, 1 - grp, act, near))
         act(send_w(p, row, grp, 2))
         pl.when(~whole(p))(lambda: act(send_w(p, row, grp, 3)))
         act(send_w(p, row, grp, 4))
@@ -203,9 +210,9 @@
     def pick(first, last):
         def choose(t):
             lend(t).wait_recv()
-            tile = grp * SHARDS + t
+            owned, held = local_of(grp * SHARDS + t)
             picked[t, :, :piece_cols] = jnp.where(
-                owned_ref[tile] == 1, adp_ref[local_ref[tile]], borrowed[t, :, :piece_cols])
+                owned, adp_ref[held], borrowed[t, :, :piece_cols])
 
         def one(t):
             choose(t)
@@ -296,12 +303,13 @@
     lax.fori_loop(0, SHARDS, swapped, 0)
 
 
-def sum_kernel(local_ref, term_ref, out_ref):
+def sum_kernel(slots_ref, term_ref, out_ref):
     out_ref[...] = jnp.zeros_like(out_ref)
     slot_count = out_ref.shape[0]
+    first = lax.axis_index("grp") * slot_count
 
     def one(t, _):
-        slot = local_ref[t]
+        slot = slots_ref[t] - first
 
         @pl.when((slot >= 0) & (slot < slot_count))
         def _():
@@ -323,9 +331,6 @@
     key_columns = cotangent.shape[1]
     shard_rows = frozen_weight.shape[0]
     halves = frozen_weight.reshape(2, shard_rows // 2, key_columns)
-    local = slots - lax.axis_index("grp") * slot_count
-    near = jnp.clip(local, 0, slot_count - 1)
-    owned = (local == near).astype(jnp.int32)
     vmem = pl.BlockSpec(memory_space=pltpu.VMEM)
     place = pl.BlockSpec(memory_space=pl.ANY)
     smem = pl.BlockSpec(memory_space=pltpu.SMEM)
@@ -338,7 +343,7 @@
             jax.ShapeDtypeStruct((rows, width), bf16),
             jax.ShapeDtypeStruct((tiles, rank, wide), bf16),
         ),
-        in_specs=[smem, smem, place, place, place, place],
+        in_specs=[smem, place, place, place, place],
         out_specs=(vmem, vmem, vmem),
         scratch_shapes=[
             pltpu.VMEM(tokens.shape, bf16),
@@ -360,7 +365,7 @@
         compiler_params=pltpu.CompilerParams(
             collective_id=0, has_side_effects=True, vmem_limit_bytes=60 * 1024 * 1024),
         name="exchange",
-    )(near, owned, tokens, cotangent, halves, adapters_t)
+    )(slots, tokens, cotangent, halves, adapters_t)
     grads = pl.pallas_call(
         sum_kernel,
         out_shape=jax.ShapeDtypeStruct((slot_count, rank, piece_cols), jnp.float32),
@@ -368,7 +373,7 @@
         out_specs=vmem,
         compiler_params=pltpu.CompilerParams(vmem_limit_bytes=24 * 1024 * 1024),
         name="slot_sums",
-    )(local, terms)
+    )(slots, terms)
     return keys, token_gradient, jnp.swapaxes(grads, 1, 2)
 
 

time: 155 us -> 148 us (0.955)
  Pallas kernels: 148 us -> 142 us
    pallas_call x1, Pallas kernels: 145 us -> 139 us  [on_block(): pl.pallas_call(exchange_kernel, out_shape=(jax.ShapeDtypeStruct((rows, ke...]
    unnamed x8 -> x10, local copies, waits for them, and re-layouts: 3.76 us -> 3.77 us
where the time goes in v7:
time: 148 us
  Pallas kernels  142 us (96%)
  local copies, waits for them, and re-layouts  3.77 us (3%)
    pallas_call x1, Pallas kernels, on_block(): pl.pallas_call(exchange_kernel, out_shape=(jax.ShapeDtypeStruct((rows, ke...  139 us
    unnamed x10, local copies, waits for them, and re-layouts  3.77 us

profile of v7, /device:TPU:0, one launch (start us, length us, event | category | flops | bytes accessed | tf_op | source)
XLA Modules:
  0.0 147.8 jit_solution(269770669572738073)
XLA Ops:
  0.6 1.4 select_reduce_fusion.slots_ref
  2.0 0.0 copy-start.1
  2.0 139.1 %exchange.1 = (bf16[128,1024]{1,0:T(8,128)(2,1)}, bf16[128,8192]{1,0:T(8,128)(2,1)}, bf16[32,64,640]{2,1,0:T(8,128)(2,1)}) custom-call(s32[32]{0:T(128)} %select_reduce_fusion.slots_ref, bf16[128,8192]{1,0:T(8,128)(2,1)} %tok_hbm.1, bf16[128,1024]{1,0:T(8,128)(2,1)} %cot_hbm.1, bf16[2,256,1024]{2,1,0:T(8,128)(2,1)} %bitcast.6, bf16[16,64,576]{2,1,0:T(8,128)(2,1)} %bitcast.5), custom_call_target="tpu_custom_call" | custom-call | tf_op jit(solution)/shard_map/exchange/pallas_call | solution.py:339
  141.1 0.0 copy-done.1
  141.1 0.0 copy-start
  141.1 1.7 %copy-done = bf16[32,64,640]{2,1,0:T(8,128)(2,1)S(1)} copy-done((bf16[32,64,640]{2,1,0:T(8,128)(2,1)S(1)}, bf16[32,64,640]{2,1,0:T(8,128)(2,1)}, u32[]{:S(2)}) %copy-start) | copy-done | bytes 2621464
  142.8 0.0 copy-start.3
  142.9 0.0 copy-start.2
  142.9 2.9 %slot_sums.1 = f32[16,64,576]{2,1,0:T(8,128)} custom-call(s32[32]{0:T(128)S(1)} %copy-done.1, bf16[32,64,640]{2,1,0:T(8,128)(2,1)S(1)} %copy-done), custom_call_target="tpu_custom_call" | custom-call | tf_op jit(solution)/shard_map/slot_sums/pallas_call | solution.py:369
  145.7 0.0 copy-done.3
  145.7 0.7 copy.11
  146.4 0.0 copy-done.2
  146.4 1.3 copy.12
Async XLA Ops:
  2.0 139.1 %copy-start.1 = (s32[32]{0:T(128)S(1)}, s32[32]{0:T(128)}, u32[]{:S(2)}) copy-start(s32[32]{0:T(128)} %select_reduce_fusion.slots_ref) | copy-start | bytes 388
  141.1 1.7 %copy-start = (bf16[32,64,640]{2,1,0:T(8,128)(2,1)S(1)}, bf16[32,64,640]{2,1,0:T(8,128)(2,1)}, u32[]{:S(2)}) copy-start(bf16[32,64,640]{2,1,0:T(8,128)(2,1)} %get-tuple-element.8.term_ref) | copy-start | bytes 7864324
  142.8 2.9 %copy-start.3 = (bf16[128,1024]{1,0:T(8,128)(2,1)S(1)}, bf16[128,1024]{1,0:T(8,128)(2,1)}, u32[]{:S(2)}) copy-start(bf16[128,1024]{1,0:T(8,128)(2,1)} %get-tuple-element.12) | copy-start | bytes 786436
  142.9 3.6 %copy-start.2 = (bf16[128,8192]{1,0:T(8,128)(2,1)S(1)}, bf16[128,8192]{1,0:T(8,128)(2,1)}, u32[]{:S(2)}) copy-start(bf16[128,8192]{1,0:T(8,128)(2,1)} %get-tuple-element.13) | copy-start | bytes 6291460

commit v8 on v7

--- a/solution.py
+++ b/solution.py
@@ -123,7 +123,7 @@
     def finish(copy):
         copy.wait_send()
 
-    near = PLANES - 2
+    near = PLANES - 3
 
     def whole(p):
         return (p == plane) | ((core == 0) & (p - plane <= near) & (plane - p <= near))

time: 148 us -> 142 us (0.959); the launches traced: 148 us -> 140 us
  Pallas kernels: 142 us -> 134 us
    pallas_call x1, Pallas kernels: 139 us -> 131 us  [on_block(): pl.pallas_call(exchange_kernel, out_shape=(jax.ShapeDtypeStruct((rows, ke...]
where the time goes in v8:
time: 142 us; the launch traced here: 140 us
  Pallas kernels  134 us (94%)
  local copies, waits for them, and re-layouts  3.77 us (3%)
    pallas_call x1, Pallas kernels, on_block(): pl.pallas_call(exchange_kernel, out_shape=(jax.ShapeDtypeStruct((rows, ke...  131 us
    unnamed x10, local copies, waits for them, and re-layouts  3.77 us
    pallas_call x1, Pallas kernels, on_block(): pl.pallas_call(sum_kernel, out_shape=jax.ShapeDtypeStruct((slot_count, ra...  2.89 us

profile of v8, /device:TPU:0, one launch (start us, length us, event | category | flops | bytes accessed | tf_op | source)
XLA Modules:
  0.0 139.8 jit_solution(10558013284531249140)
XLA Ops:
  0.6 1.4 select_reduce_fusion.slots_ref
  2.0 0.0 copy-start.1
  2.0 131.2 %exchange.1 = (bf16[128,1024]{1,0:T(8,128)(2,1)}, bf16[128,8192]{1,0:T(8,128)(2,1)}, bf16[32,64,640]{2,1,0:T(8,128)(2,1)}) custom-call(s32[32]{0:T(128)} %select_reduce_fusion.slots_ref, bf16[128,8192]{1,0:T(8,128)(2,1)} %tok_hbm.1, bf16[128,1024]{1,0:T(8,128)(2,1)} %cot_hbm.1, bf16[2,256,1024]{2,1,0:T(8,128)(2,1)} %bitcast.6, bf16[16,64,576]{2,1,0:T(8,128)(2,1)} %bitcast.5), custom_call_target="tpu_custom_call" | custom-call | tf_op jit(solution)/shard_map/exchange/pallas_call | solution.py:339
  133.2 0.0 copy-done.1
  133.2 0.0 copy-start
  133.2 1.7 %copy-done = bf16[32,64,640]{2,1,0:T(8,128)(2,1)S(1)} copy-done((bf16[32,64,640]{2,1,0:T(8,128)(2,1)S(1)}, bf16[32,64,640]{2,1,0:T(8,128)(2,1)}, u32[]{:S(2)}) %copy-start) | copy-done | bytes 2621464
  134.9 0.0 copy-start.3
  134.9 0.0 copy-start.2
  134.9 2.9 %slot_sums.1 = f32[16,64,576]{2,1,0:T(8,128)} custom-call(s32[32]{0:T(128)S(1)} %copy-done.1, bf16[32,64,640]{2,1,0:T(8,128)(2,1)S(1)} %copy-done), custom_call_target="tpu_custom_call" | custom-call | tf_op jit(solution)/shard_map/slot_sums/pallas_call | solution.py:369
  137.8 0.0 copy-done.3
  137.8 0.7 copy.11
  138.5 0.0 copy-done.2
  138.5 1.3 copy.12
Async XLA Ops:
  2.0 131.2 %copy-start.1 = (s32[32]{0:T(128)S(1)}, s32[32]{0:T(128)}, u32[]{:S(2)}) copy-start(s32[32]{0:T(128)} %select_reduce_fusion.slots_ref) | copy-start | bytes 388
  133.2 1.7 %copy-start = (bf16[32,64,640]{2,1,0:T(8,128)(2,1)S(1)}, bf16[32,64,640]{2,1,0:T(8,128)(2,1)}, u32[]{:S(2)}) copy-start(bf16[32,64,640]{2,1,0:T(8,128)(2,1)} %get-tuple-element.8.term_ref) | copy-start | bytes 7864324
  134.9 2.9 %copy-start.3 = (bf16[128,1024]{1,0:T(8,128)(2,1)S(1)}, bf16[128,1024]{1,0:T(8,128)(2,1)}, u32[]{:S(2)}) copy-start(bf16[128,1024]{1,0:T(8,128)(2,1)} %get-tuple-element.12) | copy-start | bytes 786436
  134.9 3.6 %copy-start.2 = (bf16[128,8192]{1,0:T(8,128)(2,1)S(1)}, bf16[128,8192]{1,0:T(8,128)(2,1)}, u32[]{:S(2)}) copy-start(bf16[128,8192]{1,0:T(8,128)(2,1)} %get-tuple-element.13) | copy-start | bytes 6291460
